TPU v7x, 512 devices: a whole 4x4x16 slice. The times are simulated.
512 devices in a mesh: lat: 64 (over z_lo, y, x), chan: 8 (over z_hi, core).
Axes of the slice: x: 4, y: 4, z: 16 (z_hi: 4, z_lo: 4; z = z_hi * 4 + z_lo), core: 2. Of those that a mesh axis runs over, the one named last changes fastest.
Arguments:
- ocean_state: bfloat16 [384, 256, 1440], P('lat', 'chan'), may hold values from -6 to 6
- land_mask: int32 [384, 1440], P('lat', 'chan'), may hold values 0 or 1
- order_table: int32 [384], replicated, may hold values from 0 to 383, each once
- spectral_weight: bfloat16 [384, 2, 256, 256], P('lat', None, 'chan'), may hold values from -0.25 to 0.25
- inner_weight: bfloat16 [256, 512], P(None, 'chan'), may hold values from -0.375 to 0.375
- outer_weight: bfloat16 [512, 256], P('chan'), may hold values from -0.25 to 0.25
Outputs:
- layer_output: bfloat16 [384, 1440, 256], P('lat', 'chan')
Inputs may be any that keep to these rules, and one draw needn't show every extreme that they name: `order_table`: a permutation: every order from 0 to 383 stands in exactly one slot.
All inputs are finite; a program needn't handle non-finite values. Where the computation divides by a largest or mean magnitude, that divisor is 1e-20 or more. No bound on the sum of `land_mask` on one device may be relied on, other than what follows from the above.
Results may differ from a plain program's by a relative error of at most 0.0095.
Values may be sent and summed in bfloat16 or wider, within the bound.
A program may use at most 64 MiB of HBM per device.

v0:
```python
import math

import jax
import jax.numpy as jnp
from jax import lax
from jax.sharding import PartitionSpec as P

NLAT = 384
NLON = 1440
MODES = 384


def turned_gather(arrays, axis, dims):
    turned = [jnp.moveaxis(a, dim, 0) for a, dim in zip(arrays, dims)]
    widths = [t[0].size for t in turned]
    both = jnp.concatenate([t.reshape(-1, w) for t, w in zip(turned, widths)], axis=1)
    filled = lax.all_gather(both, axis, axis=0, tiled=True)
    parts = jnp.split(filled, [sum(widths[:k]) for k in range(1, len(widths))], axis=1)
    return tuple(
        (
            jnp.moveaxis(b.reshape(-1, *t.shape[1:]), 0, dim)
            for b, t, dim in zip(parts, turned, dims)
        )
    )


def fejer_weights():
    colatitude = (jnp.arange(NLAT, dtype=jnp.float32) + 0.5) * (math.pi / NLAT)
    harmonic = jnp.arange(1, NLAT // 2 + 1).astype(jnp.float32)
    series = (
        jnp.cos(2.0 * colatitude[:, None] * harmonic[None, :])
        / (4.0 * harmonic * harmonic - 1.0)[None, :]
    )
    return 2.0 / NLAT * (1.0 - 2.0 * jnp.sum(series, axis=1))


def compose(earlier, latter):
    first_mat, first_log = earlier
    second_mat, second_log = latter
    product = jnp.stack(
        [
            second_mat[0] * first_mat[0] + second_mat[1] * first_mat[2],
            second_mat[0] * first_mat[1] + second_mat[1] * first_mat[3],
            second_mat[2] * first_mat[0] + second_mat[3] * first_mat[2],
            second_mat[2] * first_mat[1] + second_mat[3] * first_mat[3],
        ]
    )
    largest = jnp.max(jnp.abs(product), axis=0, keepdims=True)
    return (product / largest, first_log + second_log + jnp.log(largest))


def legendre_rows(order_value):
    half_rows = NLAT // 2
    colatitude = (jnp.arange(half_rows, dtype=jnp.float32) + 0.5) * (math.pi / NLAT)
    cosine = jnp.cos(colatitude)
    sine_part = jnp.sin(colatitude)
    offsets = jnp.arange(MODES).astype(jnp.float32)
    order_float = order_value.astype(jnp.float32)
    degree = order_float + offsets
    beyond_start = offsets >= 1.0
    denominator = jnp.where(beyond_start, degree * degree - order_float * order_float, 1.0)
    upper_coef = jnp.sqrt((4.0 * degree * degree - 1.0) / denominator)
    previous = degree - 1.0
    lower_coef = jnp.sqrt(
        jnp.maximum(previous * previous - order_float * order_float, 0.0)
        / jnp.maximum(4.0 * previous * previous - 1.0, 1.0)
    )
    filled = jnp.ones((MODES, half_rows), jnp.float32)
    beyond_column = beyond_start[:, None]
    matrix = jnp.stack(
        [
            jnp.where(beyond_column, upper_coef[:, None] * cosine[None, :], filled),
            jnp.where(beyond_column, -(upper_coef * lower_coef)[:, None] * filled, 0.0 * filled),
            jnp.where(beyond_column, filled, 0.0 * filled),
            jnp.where(beyond_column, 0.0 * filled, filled),
        ]
    )
    log_scale = jnp.zeros((1, MODES, half_rows), jnp.float32)
    matrix, log_scale = lax.associative_scan(compose, (matrix, log_scale), axis=1)
    steps_log = 0.5 * jnp.log((2.0 * offsets + 3.0) / (2.0 * offsets + 2.0))
    cumulative = jnp.cumsum(steps_log) - steps_log
    picked = jnp.sum(jnp.where(jnp.arange(MODES) == order_value, cumulative, 0.0 * cumulative))
    start_log = 0.5 * math.log(0.5) + picked + order_float * jnp.log(sine_part)
    northern = jnp.exp(start_log[None, :] + log_scale[0]) * matrix[0]
    northern = jnp.where((offsets < MODES - order_float)[:, None], northern, 0.0 * filled)
    parity = jnp.where(jnp.arange(MODES) % 2 == 0, 1.0, -1.0).astype(jnp.float32)
    return jnp.concatenate([northern, northern[:, ::-1] * parity[:, None]], axis=1)


def fourier_tables(orders):
    longitude = jnp.arange(NLON)
    phase_index = orders[:, None] * longitude[None, :] % NLON
    angles = phase_index.astype(jnp.float32) * (2.0 * math.pi / NLON)
    cosine = jnp.cos(angles)
    sine_part = jnp.sin(angles)
    forward = (
        jnp.concatenate([cosine, -sine_part], axis=0) * (math.sqrt(2.0 * math.pi) / NLON)
    ).astype(jnp.bfloat16)
    factor = jnp.where(orders == 0, 1.0, 2.0).astype(jnp.float32) / math.sqrt(2.0 * math.pi)
    inverse = jnp.concatenate(
        [cosine * factor[:, None], -sine_part * factor[:, None]], axis=0
    ).astype(jnp.bfloat16)
    return (forward, inverse)


def mixing_blocks(weights):
    real_part = weights[:, 0]
    imag_part = weights[:, 1]
    return jnp.stack(
        [jnp.stack([real_part, imag_part], axis=1), jnp.stack([-imag_part, real_part], axis=1)],
        axis=1,
    )


def local(ocean_state, land_mask, order_table, spectral_weight, inner_weight, outer_weight):
    local_rows = ocean_state.shape[0]
    local_channels = ocean_state.shape[1]
    slots_here = spectral_weight.shape[0]
    forward, inverse = fourier_tables(order_table)
    flat_state = ocean_state.reshape(local_rows * local_channels, NLON)
    coeffs = lax.dot_general(
        flat_state, forward, (((1,), (1,)), ((), ())), preferred_element_type=jnp.float32
    )
    coeffs = coeffs.astype(jnp.bfloat16).reshape(local_rows, local_channels, 2, MODES)
    owned_coeffs = lax.all_to_all(coeffs, "lat", split_axis=3, concat_axis=0, tiled=True)
    first_slot = lax.axis_index("lat") * slots_here
    my_orders = lax.dynamic_slice_in_dim(order_table, first_slot, slots_here)
    tables = lax.map(legendre_rows, my_orders)
    weighted = (tables * fejer_weights()[None, None, :]).astype(jnp.bfloat16)
    plain_table = tables.astype(jnp.bfloat16)
    spectra = jnp.einsum(
        "rcpm,mkr->mpck", owned_coeffs, weighted, preferred_element_type=jnp.float32
    ).astype(jnp.bfloat16)
    gathered = lax.all_gather(spectra, "chan", axis=2, tiled=True)
    blocks = mixing_blocks(spectral_weight)
    mixed_spec = jnp.einsum(
        "mpck,mpqdc->mqdk", gathered, blocks, preferred_element_type=jnp.float32
    ).astype(jnp.bfloat16)
    synthesis = jnp.einsum(
        "mqdk,mkr->rdqm", mixed_spec, plain_table, preferred_element_type=jnp.float32
    ).astype(jnp.bfloat16)
    rows_back = lax.all_to_all(synthesis, "lat", split_axis=0, concat_axis=3, tiled=True)
    spatial = jnp.dot(
        rows_back.reshape(local_rows * local_channels, 2 * MODES),
        inverse,
        preferred_element_type=jnp.float32,
    )
    spatial = spatial.reshape(local_rows, local_channels, NLON)
    hidden = (ocean_state.astype(jnp.float32) + spatial).astype(jnp.bfloat16)
    points = lax.all_to_all(hidden, "chan", split_axis=2, concat_axis=1, tiled=True)
    inner_full, outer_full = turned_gather((inner_weight, outer_weight), "chan", (1, 0))
    pre_act = jnp.einsum("rcp,ch->rph", points, inner_full, preferred_element_type=jnp.float32)
    activated = jax.nn.gelu(pre_act).astype(jnp.bfloat16)
    update = jnp.einsum("rph,hc->rpc", activated, outer_full, preferred_element_type=jnp.float32)
    ocean_mask = land_mask.astype(jnp.float32)
    residual_part = jnp.transpose(points, (0, 2, 1)).astype(jnp.float32)
    return (ocean_mask[:, :, None] * (residual_part + update)).astype(jnp.bfloat16)


def solution(mesh):
    placed = (
        P("lat", "chan", None),
        P("lat", "chan"),
        P(),
        P("lat", None, "chan", None),
        P(None, "chan"),
        P("chan", None),
    )
    return jax.shard_map(
        local, mesh=mesh, in_specs=placed, out_specs=P("lat", "chan", None), check_vma=False
    )
```

profile of v0, /device:TPU:1, one launch (start us, length us, event | category | flops | bytes accessed | tf_op | source)
XLA Modules:
  0.0 409.6 jit_solution(14290681398310745256)
XLA Ops:
  7.2 11.2 %multiply_convert_fusion.2 = (bf16[384,1440]{0,1:T(8,128)(2,1)}, bf16[384,1440]{0,1:T(8,128)(2,1)}, f32[384,1440]{0,1:T(8,128)S(1)}, f32[384,1440]{0,1:T(8,128)S(1)}) fusion(f32[384]{0:T(512)S(1)} %select_multiply_fusion, s32[384]{0:T(512)} %param.10), kind=kLoop, calls=%fused_computation.251 | loop fusion | flops 7741440 | bytes 6638592 | tf_op jit(solution)/shard_map/convert.1
  19.2 1.5 copy.33
  20.7 1.9 reshape.811
  22.6 12.8 %all-to-all-start = ((bf16[64,2,1152]{2,1,0:T(2,128)(2,1)}), bf16[64,2,1152]{2,1,0:T(2,128)(2,1)}, u32[]{:S(2)}, u32[]{:S(2)}) async-start(bf16[64,2,1152]{2,1,0:T(2,128)(2,1)} %reshape.811), calls=%async_computation | async-start | bytes 589824 | tf_op jit(solution)/shard_map/all_to_all | solution.py:125
  35.6 1.3 dynamic_slice.11
  36.9 185.9 %while.13 = (s32[]{:T(128)}, f32[6,384,384]{2,1,0:T(8,128)}, s32[6]{0:T(128)}, s32[]{:T(128)}, f32[]{:T(128)}, /*index=5*/f32[]{:T(128)}, f32[]{:T(128)}) while((s32[]{:T(128)}, f32[6,384,384]{2,1,0:T(8,128)}, s32[6]{0:T(128)}, s32[]{:T(128)}, f32[]{:T(128)}, /*index=5*/f32[]{:T(128)}, f32[]{:T(128)}) %tuple.122), condition=%wide.region_20.21_spmd, body=%wide.region_0.20_spmd.sunk | while | flops 9975949 | bytes 55190924 | solution.py:128
  36.9 1.3 dynamic_slice.13
  52.1 1.8 slice.2650
  55.1 1.4 multiply_add_fusion.111
  56.7 2.9 pad.1109
  62.9 1.4 fusion.158
  67.9 1.3 dynamic_slice.13
  83.1 1.8 slice.2650
  86.0 1.4 multiply_add_fusion.111
  87.7 2.9 pad.1109
  93.8 1.4 fusion.158
  114.1 1.8 slice.2650
  117.0 1.4 multiply_add_fusion.111
  118.6 2.9 pad.1109
  124.8 1.4 fusion.158
  145.1 1.8 slice.2650
  148.0 1.4 multiply_add_fusion.111
  149.7 2.9 pad.1109
  155.8 1.4 fusion.158
  176.1 1.8 slice.2650
  179.0 1.4 multiply_add_fusion.111
  180.7 2.9 pad.1109
  186.8 1.4 fusion.158
  207.1 1.8 slice.2650
  210.0 1.4 multiply_add_fusion.111
  211.6 2.9 pad.1109
  217.8 1.4 fusion.158
  223.9 4.1 reshape.812
  228.0 2.1 copy.35
  230.1 1.5 fusion.87
  233.3 66.6 %all-gather.2.cloned.1.call-done = bf16[6,2,256,384]{3,2,1,0:T(8,128)(2,1)} async-done(((bf16[6,2,32,384]{3,2,1,0:T(8,128)(2,1)}), bf16[6,2,256,384]{3,2,1,0:T(8,128)(2,1)}) %all-gather.2.cloned.1.call-update) | async-done | bytes 2359312 | tf_op jit(solution)/shard_map/all_gather | solution.py:134
  299.9 2.4 fusion.45
  303.4 3.2 copy.38
  307.8 21.4 %all_to_all.51 = bf16[64,2,1152]{2,1,0:T(2,128)(2,1)S(1)} all-to-all(bf16[64,2,1152]{2,1,0:T(2,128)(2,1)S(1)} %reshape.813), channel_id=1, replica_groups=mesh['lat'=64,'chan'=8] {'lat'}, dimensions={0} | all-to-all | bytes 589824 | tf_op jit(solution)/shard_map/all_to_all | solution.py:142
  330.7 3.7 fusion.44
  334.5 3.0 copy.41
  337.5 2.8 reshape.815
  340.4 7.6 %all-to-all-start.2 = ((bf16[8,2,17280]{2,1,0:T(2,128)(2,1)}), bf16[8,2,17280]{2,1,0:T(2,128)(2,1)S(1)}, u32[]{:S(2)}, u32[]{:S(2)}) async-start(bf16[8,2,17280]{2,1,0:T(2,128)(2,1)} %reshape.815), calls=%async_computation.2 | async-start | bytes 1105920 | tf_op jit(solution)/shard_map/all_to_all | solution.py:150
  348.7 43.8 %all_gather.7 = bf16[512,512]{1,0:T(8,128)(2,1)} all-gather(bf16[64,512]{1,0:T(8,128)(2,1)S(1)} %pad_maximum_fusion.33), channel_id=1, replica_groups=mesh['lat'=64,'chan'=8] {'chan'}, dimensions={0}, use_global_device_ids=true | all-gather | bytes 589824 | tf_op jit(solution)/shard_map/all_gather | solution.py:17
  392.5 2.2 reshape.816
  394.7 3.5 copy.42
  398.2 1.4 copy.43
  399.6 3.1 fusion.73
  (1590 shorter events, 130.7 us)
Async XLA Ops:
  7.2 11.3 %copy-start.32 = (bf16[6,32,1440]{2,1,0:T(8,128)(2,1)S(1)}, bf16[6,32,1440]{2,1,0:T(8,128)(2,1)}, u32[]{:S(2)}) copy-start(bf16[6,32,1440]{2,1,0:T(8,128)(2,1)} %param.8) | copy-start | bytes 1658884
  22.6 201.3 %all-to-all-start = ((bf16[64,2,1152]{2,1,0:T(2,128)(2,1)}), bf16[64,2,1152]{2,1,0:T(2,128)(2,1)}, u32[]{:S(2)}, u32[]{:S(2)}) async-start(bf16[64,2,1152]{2,1,0:T(2,128)(2,1)} %reshape.811), calls=%async_computation | async-start | bytes 589824 | tf_op jit(solution)/shard_map/all_to_all | solution.py:125
  35.4 264.6 %all-gather.2.cloned.1.call-start = ((), (), s32[]{:S(2)}) async-start(), calls=%async_computation.3 | async-start | bytes 2654208 | tf_op jit(solution)/shard_map/all_gather | solution.py:134
  59.8 1.3 copy-start.22
  59.8 1.3 copy-start.29
  59.8 1.3 copy-start.27
  59.8 1.4 copy-start.25
  59.8 1.5 copy-start.18
  59.8 1.7 copy-start.14
  60.6 1.3 copy-start.5
  90.8 1.3 copy-start.22
  90.8 1.3 copy-start.29
  90.8 1.3 copy-start.27
  90.8 1.4 copy-start.25
  90.8 1.5 copy-start.18
  90.8 1.7 copy-start.14
  91.5 1.3 copy-start.5
  121.7 1.3 copy-start.22
  121.7 1.3 copy-start.29
  121.7 1.3 copy-start.27
  121.7 1.4 copy-start.25
  121.8 1.5 copy-start.18
  121.8 1.7 copy-start.14
  122.5 1.3 copy-start.5
  152.7 1.3 copy-start.22
  152.7 1.3 copy-start.29
  152.8 1.3 copy-start.27
  152.8 1.4 copy-start.25
  152.8 1.5 copy-start.18
  152.8 1.7 copy-start.14
  153.5 1.3 copy-start.5
  183.7 1.3 copy-start.29
  183.7 1.3 copy-start.27
  183.8 1.4 copy-start.25
  183.8 1.5 copy-start.18
  183.8 1.7 copy-start.14
  184.5 1.3 copy-start.5
  214.7 1.3 copy-start.29
  214.7 1.3 copy-start.27
  214.7 1.4 copy-start.25
  214.7 1.5 copy-start.18
  214.8 1.7 copy-start.14
  215.5 1.3 copy-start.5
  222.8 7.3 %copy-start.6 = (f32[6,384,384]{2,1,0:T(8,128)S(1)}, f32[6,384,384]{2,1,0:T(8,128)}, u32[]{:S(2)}) copy-start(f32[6,384,384]{2,1,0:T(8,128)} %get-tuple-element.65) | copy-start | bytes 10616836
  337.5 10.4 %copy-start.31 = (s32[6,180]{1,0:T(8,128)S(1)}, s32[6,180]{1,0:T(8,128)}, u32[]{:S(2)}) copy-start(s32[6,180]{1,0:T(8,128)} %param.9) | copy-start | bytes 12964
  337.5 10.4 %copy-start.30 = (bf16[64,256]{1,0:T(8,128)(2,1)S(1)}, bf16[64,256]{1,0:T(8,128)(2,1)}, u32[]{:S(2)}) copy-start(bf16[64,256]{1,0:T(8,128)(2,1)} %param.13) | copy-start | bytes 98308
  340.4 52.2 %all-to-all-start.2 = ((bf16[8,2,17280]{2,1,0:T(2,128)(2,1)}), bf16[8,2,17280]{2,1,0:T(2,128)(2,1)S(1)}, u32[]{:S(2)}, u32[]{:S(2)}) async-start(bf16[8,2,17280]{2,1,0:T(2,128)(2,1)} %reshape.815), calls=%async_computation.2 | async-start | bytes 1105920 | tf_op jit(solution)/shard_map/all_to_all | solution.py:150
  394.7 4.9 %copy-start.23 = (bf16[512,512]{1,0:T(8,128)(2,1)S(1)}, bf16[512,512]{1,0:T(8,128)(2,1)}, u32[]{:S(2)}) copy-start(bf16[512,512]{1,0:T(8,128)(2,1)} %all_gather.7) | copy-start | bytes 1572868
  (128 other events, 99.8 us)
Sparse Core Ops, SparseCore 0:
  231.7 68.1 all-gather.1
where the time goes:
time: 411 us; the launch traced here: 410 us
  local copies, waits for them, and re-layouts  143 us (35%)
  other arithmetic  71.4 us (17%)
  waiting for transfers between devices  66.7 us (16%)
  blocking collectives  65.2 us (16%)
  starting transfers between devices  20.6 us (5%)
  loops' own time  16.7 us (4%)
  between operations  13.6 us (3%)
  matrix products  12.5 us (3%)
    while x354, local copies, waits for them, and re-layouts  66.9 us
    all_gather x1, waiting for transfers between devices, local(): gathered = lax.all_gather(spectra, 'chan', axis=2, tiled=True)  66.6 us
    all_gather x1, blocking collectives, turned_gather(): filled = lax.all_gather(both, axis, axis=0, tiled=True)  43.8 us
    slice x318, local copies, waits for them, and re-layouts, legendre_rows(): lax.associative_scan(compose, (matrix, log_scale), axis=1)  28.7 us
    all_to_all x1, blocking collectives, local(): lax.all_to_all(synthesis, 'lat', split_axis=0, concat_axis=3, tiled=True)  21.4 us
    another operation x1, loops' own time, local(): tables = lax.map(legendre_rows, my_orders)  16.7 us
    another operation x13, other arithmetic  13.3 us
    unnamed x16, local copies, waits for them, and re-layouts  12.8 us
  transfers between devices with their start and end apart: 3, of which 1 were waited for; matrix products, arithmetic and copies ran while one was open for 32% of the time, Pallas kernels for 0%

commit v1 on v0

v1 whole, which is shorter than its diff:
```python
import functools
import math

import jax
import jax.numpy as jnp
import ml_dtypes
import numpy as np
from jax import lax
from jax.experimental import pallas as pl
from jax.experimental.pallas import tpu as pltpu
from jax.sharding import PartitionSpec as P

NLAT = 384
NLON = 1440
MODES = 384
ZL, YX, CH = 4, 16, 8
SLOTS = 6
ROWS = 6
CHANS = 32
PTS = 96
HALF = 90
LANES = 2 * ROWS * CHANS
BLOCK = 2 * ZL * ROWS
WIDE = YX * BLOCK
GROUPS = WIDE // 128
BF = jnp.bfloat16
F32 = jnp.float32


def bf(a):
    return np.asarray(a, np.float32).astype(ml_dtypes.bfloat16)


@functools.lru_cache(None)
def constants():
    m, j = np.arange(MODES), np.arange(NLON)
    angle = 2 * np.pi * ((m[:, None] * j[None, :]) % NLON) / NLON
    waves = np.stack([np.cos(angle), -np.sin(angle)])
    fwd = bf((waves * (math.sqrt(2 * np.pi) / NLON)).reshape(2 * MODES, NLON))
    factor = np.where(m == 0, 1.0, 2.0) / math.sqrt(2 * np.pi)
    inv = (waves * factor[None, :, None]).reshape(2, MODES, CH, 2, HALF)
    inv = inv.transpose(3, 2, 4, 0, 1)
    inv = np.pad(inv, ((0, 0), (0, 0), (0, PTS - HALF), (0, 0), (0, 0)))
    inv = bf(inv.reshape(2, CH * PTS, 2 * MODES))
    spread = np.zeros((2, CH, PTS, NLON), np.float32)
    for half in range(2):
        for c in range(CH):
            for t in range(HALF):
                spread[half, c, t, 180 * c + HALF * half + t] = 1
    spread = bf(spread.reshape(2, CH * PTS, NLON))
    perm = np.zeros((WIDE, WIDE), np.float32)
    yx, p, zl, r = np.meshgrid(
        np.arange(YX), np.arange(2), np.arange(ZL), np.arange(ROWS), indexing="ij"
    )
    target = ((yx * 2 + p) * ZL + zl) * ROWS + r
    source = ((p * ROWS + r) * ZL + zl) * YX + yx
    perm[target.ravel(), source.ravel()] = 1
    row = (zl * YX + yx) * ROWS + r
    theta_all = (np.arange(NLAT) + 0.5) * np.pi / NLAT
    h = np.arange(1, NLAT // 2 + 1)
    series = np.cos(2 * theta_all[:, None] * h) / (4.0 * h * h - 1)
    quad_all = 2.0 / NLAT * (1 - 2 * series.sum(1))
    theta = theta_all[row.ravel()]
    geo = np.zeros((2, 8, 128), np.float32)
    geo[0, :GROUPS] = np.cos(theta).reshape(GROUPS, 128)
    geo[1, :GROUPS] = np.log(np.sin(theta)).reshape(GROUPS, 128)
    quad = np.stack([quad_all[row.ravel()] * (p.ravel() == k) for k in range(2)])
    q = np.arange(1, MODES)
    cum = np.concatenate([[0.0], np.cumsum(0.5 * np.log((2.0 * q + 1) / (2.0 * q)))])
    return (
        fwd,
        inv,
        spread,
        bf(perm),
        bf(perm.T),
        geo,
        quad.astype(np.float32),
        cum.astype(np.float32)[None],
    )


def dot(a, b, ca=1, cb=0):
    return lax.dot_general(a, b, (((ca,), (cb,)), ((), ())), preferred_element_type=F32)


def spectral(
    ord_s, ord_c, ord_l, x, geo, quad, cum, fwd_h, inv_h, spread_h, perm_h, permt_h, w_h,
    out,
    fwd, inv, spread, perm, permt, wk, s1, r1, tmp, s2, r2, mix, s3, r3, tmp2, s4, r4, ym, xt, s5, r5,
    acoef, ucoef, table, weighted, plain_t,
    lsem, wsend, wrecv, s1s, s1r, s2s, s2r, s3s, s3r, s4s, s4r, s5s, s5r,
):
    lat, ch = lax.axis_index("lat"), lax.axis_index("chan")
    zl, yx = lat // YX, lax.rem(lat, YX)
    active = lax.rem(ch, 4) != 3
    slot = ch - ch // 4

    def chan_of(s):
        return s + s // 3

    def z_peer(i):
        return (i // CH) * YX + yx, lax.rem(i, CH)

    def z_holder(i):
        return (i // SLOTS) * YX + yx, chan_of(lax.rem(i, SLOTS))

    def xy_peer(i):
        return zl * YX + i, ch

    def chan_peer(i):
        return lat, i

    def chan_holder(i):
        return lat, chan_of(i)

    def remote(src, dst, ssem, rsem, to):
        return pltpu.make_async_remote_copy(
            src_ref=src, dst_ref=dst, send_sem=ssem, recv_sem=rsem,
            device_id=to, device_id_type=pl.DeviceIdType.MESH,
        )

    def send(n, start, peer, src, dst, ssem, rsem):
        def body(i, carry):
            t = lax.rem(i + start, n)
            to = peer(t)
            mine = (to[0] == lat) & (to[1] == ch)

            @pl.when(jnp.logical_not(mine))
            def _():
                remote(src(t), dst, ssem.at[t], rsem, to).start()

            @pl.when(mine)
            def _():
                pltpu.make_async_copy(src(t), dst, rsem).start()

            return carry

        lax.fori_loop(0, n, body, 0)

    def sent(n, peer, src, dst, ssem, rsem):
        def body(t, carry):
            to = peer(t)

            @pl.when((to[0] != lat) | (to[1] != ch))
            def _():
                remote(src(t), dst, ssem.at[t], rsem, to).wait_send()

            return carry

        lax.fori_loop(0, n, body, 0)

    def received(n, dst, rsem):
        def body(t, carry):
            pltpu.make_async_copy(dst(t), dst(t), rsem.at[t]).wait()
            return carry

        lax.fori_loop(0, n, body, 0)

    loads = [
        pltpu.make_async_copy(a, b, lsem.at[k])
        for k, (a, b) in enumerate(
            ((fwd_h, fwd), (perm_h, perm), (spread_h, spread), (permt_h, permt), (inv_h, inv))
        )
    ]
    for load in loads:
        load.start()

    barrier = pltpu.get_barrier_semaphore()

    def greet(n, peer):
        def body(i, carry):
            to = peer(i)

            @pl.when((to[0] != lat) | (to[1] != ch))
            def _():
                pl.semaphore_signal(
                    barrier, inc=1, device_id=to, device_id_type=pl.DeviceIdType.MESH
                )

            return carry

        lax.fori_loop(0, n, body, 0)

    greet(ZL * CH, z_peer)
    greet(YX, xy_peer)

    loads[0].wait()
    parts = [dot(fwd[k * MODES : (k + 1) * MODES, :], x[...], 1, 1) for k in range(2)]
    coeffs = jnp.concatenate(parts, axis=1).astype(BF)
    natural = lax.broadcasted_iota(jnp.int32, (MODES, MODES), 1)
    select = jnp.where(natural == ord_c[...], 1.0, 0.0).astype(BF)
    s1[...] = dot(select, coeffs).astype(BF).reshape(ZL * SLOTS, YX, LANES)

    pl.semaphore_wait(barrier, ZL * CH - 1 + YX - 1)
    me_z = zl * CH + ch
    me_slot = zl * SLOTS + slot
    send(ZL * SLOTS, zl * SLOTS + lax.rem(ch, SLOTS), z_holder,
         lambda t: s1.at[t], r1.at[me_z], s1s, s1r.at[me_z])
    send(SLOTS, lax.rem(ch, SLOTS), chan_holder,
         lambda t: w_h.at[t], wk.at[ch], wsend, wrecv.at[ch])

    loads[2].wait()
    for half in range(2):
        xt[half] = dot(spread[half], x[...], 1, 1).astype(BF)

    @pl.when(active)
    def _():
        order = ord_s[lat * SLOTS + slot].astype(F32)
        i = lax.broadcasted_iota(jnp.int32, (MODES, 128), 0).astype(F32)
        later = i >= 1.0
        degree = order + i
        low = i - 1.0
        prev = degree - 1.0
        a = jnp.sqrt(
            (4.0 * degree * degree - 1.0) / jnp.where(later, i * (2.0 * order + i), 1.0)
        )
        b = jnp.sqrt(
            jnp.maximum(low * (2.0 * order + low), 0.0)
            / jnp.maximum(4.0 * prev * prev - 1.0, 1.0)
        )
        acoef[...] = jnp.where(later, a, 0.0)
        ucoef[...] = jnp.where(later, a * b, 1.0)
        m_of = lax.broadcasted_iota(jnp.int32, (1, MODES), 1).astype(F32)
        picked = jnp.sum(jnp.where(m_of == order, cum[...], 0.0), axis=1, keepdims=True)
        cosine = geo[0]
        log_first = order * geo[1] + (picked + 0.5 * math.log(0.5))

        def steps(t, carry):
            one, two, log_now = carry
            factor = jnp.exp(log_now)
            for s in range(8):
                k = t * 8 + s
                now = acoef[pl.ds(k, 1), :] * cosine * one - ucoef[pl.ds(k, 1), :] * two
                table[pl.ds(pl.multiple_of(k * 8, 8), 8), :] = now * factor
                one, two = now, one
            big = jnp.maximum(jnp.abs(one), jnp.abs(two)) > 2.0**40
            shrink = jnp.where(big, 2.0**-40, 1.0)
            log_now = log_now + jnp.where(big, 40.0 * math.log(2.0), 0.0)
            return one * shrink, two * shrink, log_now

        lax.fori_loop(
            0, MODES // 8, steps,
            (jnp.zeros((8, 128), F32), jnp.full((8, 128), -1.0, F32), log_first),
        )
        valid = i < MODES - order
        for g in range(GROUPS):
            lanes = slice(g * 128, (g + 1) * 128)
            part = jnp.where(valid, table[pl.ds(g, MODES, stride=8), :], 0.0)
            for p in range(2):
                weighted[p, :, lanes] = (part * quad[p : p + 1, lanes]).astype(BF)
            turned = part.T
            row = lax.broadcasted_iota(jnp.int32, (128, MODES), 0) + g * 128
            which = lax.rem(row // (BLOCK // 2), 2)
            for p in range(2):
                plain_t[lanes, p * MODES : (p + 1) * MODES] = jnp.where(
                    which == p, turned, 0.0
                ).astype(BF)

        received(ZL * CH, lambda t: r1.at[t], s1r)
        blocks = [
            jnp.concatenate([r1[z * CH + c] for z in range(ZL)], axis=0) for c in range(CH)
        ]
        for k in range(2 * ROWS):
            tmp[k * ZL * YX : (k + 1) * ZL * YX, :] = jnp.concatenate(
                [blocks[c][:, k * CHANS : (k + 1) * CHANS] for c in range(CH)], axis=1
            )
        loads[1].wait()
        s2[...] = dot(perm[...], tmp[...]).astype(BF).reshape(YX, BLOCK, CH * CHANS)
        send(YX, yx, xy_peer, lambda t: s2.at[t], r2.at[yx], s2s, s2r.at[yx])
        received(CH, lambda t: wk.at[t], wrecv)
        received(YX, lambda t: r2.at[t], s2r)
        field = r2[...].reshape(WIDE, CH * CHANS)
        real, imag = (dot(weighted[p], field).astype(BF) for p in range(2))
        w_real = wk[:, 0].reshape(CH * CHANS, CH * CHANS)
        w_imag = wk[:, 1].reshape(CH * CHANS, CH * CHANS)
        mix[0:MODES, :] = (dot(real, w_real, 1, 1) - dot(imag, w_imag, 1, 1)).astype(BF)
        mix[MODES:, :] = (dot(real, w_imag, 1, 1) + dot(imag, w_real, 1, 1)).astype(BF)
        s3[...] = dot(plain_t[...], mix[...]).astype(BF).reshape(YX, BLOCK, CH * CHANS)
        send(YX, yx, xy_peer, lambda t: s3.at[t], r3.at[yx], s3s, s3r.at[yx])
        loads[3].wait()
        received(YX, lambda t: r3.at[t], s3r)
        tmp2[...] = dot(permt[...], r3[...].reshape(WIDE, CH * CHANS)).astype(BF)
        for c in range(CH):
            piece = jnp.concatenate(
                [
                    tmp2[k * ZL * YX : (k + 1) * ZL * YX, c * CHANS : (c + 1) * CHANS]
                    for k in range(2 * ROWS)
                ],
                axis=1,
            )
            for z in range(ZL):
                s4[z * CH + c] = piece[z * YX : (z + 1) * YX, :]
        send(ZL * CH, me_z, z_peer, lambda t: s4.at[t], r4.at[me_slot], s4s, s4r.at[me_slot])

    @pl.when(jnp.logical_not(active))
    def _():
        loads[1].wait()
        loads[3].wait()

    slot_of = lax.broadcasted_iota(jnp.int32, (MODES, MODES), 0)
    unselect = jnp.where(slot_of == ord_l[...], 1.0, 0.0).astype(BF)
    loads[4].wait()
    received(ZL * SLOTS, lambda t: r4.at[t], s4r)
    held = dot(unselect, r4[...].reshape(MODES, LANES)).astype(BF)
    ym[0:MODES, :] = held[:, : LANES // 2]
    ym[MODES:, :] = held[:, LANES // 2 :]
    halves = [
        (dot(inv[half], ym[...]) + xt[half].astype(F32)).astype(BF) for half in range(2)
    ]
    s5[...] = jnp.concatenate(halves, axis=1).reshape(CH, PTS, LANES)
    send(CH, ch, chan_peer, lambda t: s5.at[t], r5.at[ch], s5s, s5r.at[ch])
    received(CH, lambda t: r5.at[t], s5r)
    out[...] = r5[...]

    sent(ZL * SLOTS, z_holder, lambda t: s1.at[t], r1.at[me_z], s1s, s1r.at[me_z])
    sent(SLOTS, chan_holder, lambda t: w_h.at[t], wk.at[ch], wsend, wrecv.at[ch])

    @pl.when(active)
    def _():
        sent(YX, xy_peer, lambda t: s2.at[t], r2.at[yx], s2s, s2r.at[yx])
        sent(YX, xy_peer, lambda t: s3.at[t], r3.at[yx], s3s, s3r.at[yx])
        sent(ZL * CH, z_peer, lambda t: s4.at[t], r4.at[me_slot], s4s, s4r.at[me_slot])

    sent(CH, chan_peer, lambda t: s5.at[t], r5.at[ch], s5s, s5r.at[ch])


def spectral_call(order_table, flat_state, spectral_weight):
    fwd, inv, spread, perm, permt, geo, quad, cum = constants()
    slots = order_table.reshape(ZL, YX, SLOTS).transpose(0, 2, 1).reshape(-1)
    vmem = pl.BlockSpec(memory_space=pltpu.VMEM)
    anywhere = pl.BlockSpec(memory_space=pl.ANY)
    sem = pltpu.SemaphoreType.DMA
    full = CH * CHANS
    return pl.pallas_call(
        spectral,
        out_shape=jax.ShapeDtypeStruct((CH, PTS, LANES), BF),
        in_specs=[pl.BlockSpec(memory_space=pltpu.SMEM)] + [vmem] * 6 + [anywhere] * 6,
        out_specs=vmem,
        scratch_shapes=[
            pltpu.VMEM(fwd.shape, BF),
            pltpu.VMEM(inv.shape, BF),
            pltpu.VMEM(spread.shape, BF),
            pltpu.VMEM(perm.shape, BF),
            pltpu.VMEM(perm.shape, BF),
            pltpu.VMEM((CH, 2, CHANS, full), BF),
            pltpu.VMEM((ZL * SLOTS, YX, LANES), BF),
            pltpu.VMEM((ZL * CH, YX, LANES), BF),
            pltpu.VMEM((WIDE, full), BF),
            pltpu.VMEM((YX, BLOCK, full), BF),
            pltpu.VMEM((YX, BLOCK, full), BF),
            pltpu.VMEM((2 * MODES, full), BF),
            pltpu.VMEM((YX, BLOCK, full), BF),
            pltpu.VMEM((YX, BLOCK, full), BF),
            pltpu.VMEM((WIDE, full), BF),
            pltpu.VMEM((ZL * CH, YX, LANES), BF),
            pltpu.VMEM((ZL * SLOTS, YX, LANES), BF),
            pltpu.VMEM((2 * MODES, LANES // 2), BF),
            pltpu.VMEM((2, CH * PTS, LANES // 2), BF),
            pltpu.VMEM((CH, PTS, LANES), BF),
            pltpu.VMEM((CH, PTS, LANES), BF),
            pltpu.VMEM((MODES, 128), F32),
            pltpu.VMEM((MODES, 128), F32),
            pltpu.VMEM((MODES * 8, 128), F32),
            pltpu.VMEM((2, MODES, WIDE), BF),
            pltpu.VMEM((WIDE, 2 * MODES), BF),
            sem((5,)),
            sem((SLOTS,)),
            sem((CH,)),
            sem((ZL * SLOTS,)),
            sem((ZL * CH,)),
            sem((YX,)),
            sem((YX,)),
            sem((YX,)),
            sem((YX,)),
            sem((ZL * CH,)),
            sem((ZL * SLOTS,)),
            sem((CH,)),
            sem((CH,)),
        ],
        compiler_params=pltpu.CompilerParams(
            collective_id=0, has_side_effects=True, vmem_limit_bytes=48 * 2**20
        ),
        cost_estimate=pl.CostEstimate(
            flops=2 * 10**9, bytes_accessed=12 * 10**6, transcendentals=10**5
        ),
    )(
        order_table, slots[:, None], slots[None, :], flat_state, geo, quad, cum,
        fwd, inv, spread, perm, permt, spectral_weight,
    )


def mlp(field, weights, out):
    inner = weights[:, :64, :].reshape(512, 256)
    outer = weights[:, 64:, :].reshape(512, 256)
    for k in range(2 * ROWS):
        hidden = jnp.concatenate(
            [field[c, :, k * CHANS : (k + 1) * CHANS] for c in range(CH)], axis=1
        )
        activated = jax.nn.gelu(dot(hidden, inner, 1, 1)).astype(BF)
        out[k] = (hidden.astype(F32) + dot(activated, outer)).astype(BF)


def local(ocean_state, land_mask, order_table, spectral_weight, inner_weight, outer_weight):
    own = jnp.concatenate([inner_weight.T, outer_weight], axis=0)
    weights = lax.all_gather(own, "chan", axis=0)
    flat_state = ocean_state.reshape(ROWS * CHANS, NLON)
    field = spectral_call(order_table, flat_state, spectral_weight)
    points = pl.pallas_call(
        mlp,
        out_shape=jax.ShapeDtypeStruct((2 * ROWS, PTS, 256), BF),
        compiler_params=pltpu.CompilerParams(vmem_limit_bytes=32 * 2**20),
    )(field, weights)
    points = points.reshape(2, ROWS, PTS, 256)[:, :, :HALF].transpose(1, 0, 2, 3)
    points = points.reshape(ROWS, 2 * HALF, 256)
    return (land_mask.astype(F32)[:, :, None] * points.astype(F32)).astype(BF)


def solution(mesh):
    placed = (
        P("lat", "chan", None),
        P("lat", "chan"),
        P(),
        P("lat", None, "chan", None),
        P(None, "chan"),
        P("chan", None),
    )
    return jax.shard_map(
        local, mesh=mesh, in_specs=placed, out_specs=P("lat", "chan", None), check_vma=False
    )
```

time: 411 us -> 141 us (0.34)
  local copies, waits for them, and re-layouts: 143 us -> 9.1 us
  Pallas kernels: 0 us -> 111 us
  other arithmetic: 71.4 us -> 1.14 us
  waiting for transfers between devices: 66.7 us -> 0 us
  blocking collectives: 65.2 us -> 18.2 us
  starting transfers between devices: 20.6 us -> 0 us
  loops' own time: 16.7 us -> 0 us
  between operations: 13.6 us -> 0.09 us
  matrix products: 12.5 us -> 0 us
    pallas_call x0 -> x2, Pallas kernels: none -> 111 us  [the longest x1 109 us: spectral_call(): pl.pallas_call(spectral, out_shape=jax.ShapeDtypeStruct((CH, PTS, LANES),...]
    while x354 -> x0, local copies, waits for them, and re-layouts: 66.9 us -> none
    all_gather x1 -> x0, waiting for transfers between devices: 66.6 us -> none  [local(): gathered = lax.all_gather(spectra, 'chan', axis=2, tiled=True)]
    slice x318 -> x0, local copies, waits for them, and re-layouts: 28.7 us -> none  [legendre_rows(): lax.associative_scan(compose, (matrix, log_scale), axis=1)]
    all_gather x1, blocking collectives: 43.8 us -> 18.2 us  [local(): weights = lax.all_gather(own, 'chan', axis=0)]
    add x312 -> x0, other arithmetic: 21.8 us -> none  [the longest x96 11 us: compose(): second_mat[0] * first_mat[0] + second_mat[1] * first_mat[2]]
    all_to_all x1 -> x0, blocking collectives: 21.4 us -> none  [local(): lax.all_to_all(synthesis, 'lat', split_axis=0, concat_axis=3, tiled=True)]
    all_to_all x2 -> x0, starting transfers between devices: 20.3 us -> none  [the longest x1 12.8 us: local(): lax.all_to_all(coeffs, 'lat', split_axis=3, concat_axis=0, tiled=True)]
  transfers between devices with their start and end apart: 3 -> 0, of which waited for: 1 -> 0; matrix products, arithmetic and copies ran while one was open for 32% -> 0% of each run, Pallas kernels for 0% -> 0%
where the time goes in v1:
time: 141 us; the launch traced here: 140 us
  Pallas kernels  111 us (79%)
  blocking collectives  18.2 us (13%)
  local copies, waits for them, and re-layouts  9.1 us (6%)
    pallas_call x1, Pallas kernels, spectral_call(): pl.pallas_call(spectral, out_shape=jax.ShapeDtypeStruct((CH, PTS, LANES),...  109 us
    all_gather x1, blocking collectives, local(): weights = lax.all_gather(own, 'chan', axis=0)  18.2 us
    unnamed x22, local copies, waits for them, and re-layouts  7.86 us

profile of v1, /device:TPU:1, one launch (start us, length us, event | category | flops | bytes accessed | tf_op | source)
XLA Modules:
  0.0 139.7 jit_solution(13987111797940153082)
XLA Ops:
  0.0 0.8 reshape.13
  0.8 0.1 copy.16
  0.9 0.1 broadcast_in_dim_reshape.8.ord_c
  1.1 0.1 broadcast_in_dim_reshape.7.ord_l
  1.1 0.0 copy-start
  1.1 1.3 copy-done
  2.4 0.0 copy-start.1
  2.4 1.3 copy-done.1
  3.7 0.0 copy-start.2
  3.7 1.1 copy-done.2
  4.7 0.0 copy-start.3
  4.8 0.9 copy-done.3
  5.7 0.0 copy-start.4
  5.7 0.7 copy-done.4
  6.4 0.0 copy-start.5
  6.4 0.7 copy-done.5
  7.1 0.0 copy-start.6
  7.1 0.7 copy-done.6
  7.7 0.0 copy-start.7
  7.7 0.7 copy-done.7
  8.4 0.0 copy-start.8
  8.4 0.0 copy-start.9
  8.4 108.5 %shard_map.136.field = bf16[8,96,384]{2,1,0:T(8,128)(2,1)S(1)} custom-call(s32[384]{0:T(512)S(1)} %copy-done.4, s32[384,1]{1,0:T(8,128)S(1)} %broadcast_in_dim_reshape.8.ord_c, s32[1,384]{1,0:T(1,128)S(1)} %broadcast_in_dim_reshape.7.ord_l, bf16[192,1440]{1,0:T(8,128)(2,1)S(1)} %bitcast.9, f32[2,8,128]{2,1,0:T(8,128)S(1)} %copy-done.5, ...), custom_call_target="tpu_custom_call" | custom-call | flops 2000000000 | bytes 12000000 | tf_op jit(solution)/shard_map/pallas_call | solution.py:334
  117.0 0.0 copy-done.8
  117.0 0.0 copy-done.9
  117.0 18.2 %all-gather = bf16[1024,256]{1,0:T(8,128)(2,1)S(1)} all-gather(bf16[128,256]{1,0:T(8,128)(2,1)S(1)} %pad_maximum_fusion), channel_id=2, replica_groups=mesh['lat'=64,'chan'=8] {'chan'}, dimensions={0}, use_global_device_ids=true | all-gather | bytes 589824 | tf_op jit(solution)/shard_map/all_gather | solution.py:405
  135.2 2.7 %shard_map.137 = bf16[12,96,256]{2,1,0:T(8,128)(2,1)S(1)} custom-call(bf16[8,96,384]{2,1,0:T(8,128)(2,1)S(1)} %shard_map.136.field, bf16[8,128,256]{2,1,0:T(8,128)(2,1)S(1)} %bitcast.8), custom_call_target="tpu_custom_call" | custom-call | tf_op jit(solution)/shard_map/pallas_call | solution.py:408
  137.9 0.1 convert_bitcast_fusion
  138.0 0.0 copy-start.10
  138.0 0.1 reshape.16
  138.1 0.6 copy-done.10
  138.7 1.0 multiply_convert_fusion
  (2 shorter events, 0.0 us)
Async XLA Ops:
  1.1 1.3 copy-start
  2.4 1.3 copy-start.1
  3.7 1.1 copy-start.2
  4.7 0.9 copy-start.3
  5.7 0.7 copy-start.4
  6.4 0.7 copy-start.5
  7.1 0.7 copy-start.6
  7.7 0.7 copy-start.7
  8.4 108.6 %copy-start.8 = (bf16[64,256]{1,0:T(8,128)(2,1)S(1)}, bf16[64,256]{1,0:T(8,128)(2,1)}, u32[]{:S(2)}) copy-start(bf16[64,256]{1,0:T(8,128)(2,1)} %param.19) | copy-start | bytes 98308
  8.4 108.6 %copy-start.9 = (bf16[256,64]{0,1:T(8,128)(2,1)S(1)}, bf16[256,64]{0,1:T(8,128)(2,1)}, u32[]{:S(2)}) copy-start(bf16[256,64]{0,1:T(8,128)(2,1)} %param.18) | copy-start | bytes 98308
  138.0 0.7 copy-start.10

commit v2 on v1

v2 whole, which is shorter than its diff:
```python
import functools
import math

import jax
import jax.numpy as jnp
import ml_dtypes
import numpy as np
from jax import lax
from jax.experimental import pallas as pl
from jax.experimental.pallas import tpu as pltpu
from jax.sharding import PartitionSpec as P

NLAT = 384
NLON = 1440
MODES = 384
ZL, YX, CH = 4, 16, 8
SLOTS = 6
ROWS, CHANS, FFN = 6, 32, 512
FULL = CH * CHANS
GROUPS, PAIR = 3, 2
PTS = 96
HALF = 90
LANES = 2 * PAIR * CHANS
BLOCK = 2 * ZL * PAIR
WIDE = YX * BLOCK
TILES = YX
BF = jnp.bfloat16
F32 = jnp.float32


def bf(a):
    return np.asarray(a, np.float32).astype(ml_dtypes.bfloat16)


@functools.lru_cache(None)
def constants():
    m, j = np.arange(MODES), np.arange(NLON)
    angle = 2 * np.pi * ((m[:, None] * j[None, :]) % NLON) / NLON
    waves = np.stack([np.cos(angle), -np.sin(angle)])
    fwd = bf((waves * (math.sqrt(2 * np.pi) / NLON)).reshape(2 * MODES, NLON))
    factor = np.where(m == 0, 1.0, 2.0) / math.sqrt(2 * np.pi)
    inv = (waves * factor[None, :, None]).reshape(2, MODES, CH, 2, HALF)
    inv = inv.transpose(3, 2, 4, 0, 1)
    inv = np.pad(inv, ((0, 0), (0, 0), (0, PTS - HALF), (0, 0), (0, 0)))
    inv = bf(inv.reshape(2, CH * PTS, 2 * MODES))
    spread = np.zeros((2, CH, PTS, NLON), np.float32)
    for half in range(2):
        for c in range(CH):
            for t in range(HALF):
                spread[half, c, t, 180 * c + HALF * half + t] = 1
    spread = bf(spread.reshape(2, CH * PTS, NLON))
    perm = np.zeros((WIDE, WIDE), np.float32)
    yx, p, zl, r = np.meshgrid(
        np.arange(YX), np.arange(2), np.arange(ZL), np.arange(PAIR), indexing="ij"
    )
    target = ((yx * 2 + p) * ZL + zl) * PAIR + r
    source = ((p * PAIR + r) * ZL + zl) * YX + yx
    perm[target.ravel(), source.ravel()] = 1
    slots = np.arange(MODES).reshape(ZL, YX, SLOTS).transpose(0, 2, 1).ravel()
    shuffle = np.zeros((MODES, MODES), np.float32)
    shuffle[np.arange(MODES), slots] = 1
    first = (zl * YX + yx) * ROWS + r
    row = np.concatenate([(first + PAIR * g).ravel() for g in range(GROUPS)])
    part = np.tile(p.ravel(), GROUPS)
    theta_all = (np.arange(NLAT) + 0.5) * np.pi / NLAT
    h = np.arange(1, NLAT // 2 + 1)
    series = np.cos(2 * theta_all[:, None] * h) / (4.0 * h * h - 1)
    quad_all = 2.0 / NLAT * (1 - 2 * series.sum(1))
    theta = theta_all[row]
    q = np.arange(1, MODES)
    aux = np.zeros((32, GROUPS * WIDE), np.float32)
    aux[0:6, :128] = np.cos(theta).reshape(6, 128)
    aux[8:14, :128] = np.log(np.sin(theta)).reshape(6, 128)
    aux[16] = quad_all[row] * (part == 0)
    aux[17] = quad_all[row] * (part == 1)
    aux[24, 1:MODES] = np.cumsum(0.5 * np.log((2.0 * q + 1) / (2.0 * q)))
    return fwd, inv, spread, bf(perm), bf(perm.T), bf(shuffle), aux


def dot(a, b, ca=1, cb=0):
    return lax.dot_general(a, b, (((ca,), (cb,)), ((), ())), preferred_element_type=F32)


def layer(
    ord_v, mask, x_h, aux_h, fwd_h, shuffle_h, perm_h, permt_h, spread_h, inv_h, w_h, inner_h, outer_h,
    out,
    x, aux, fwd, shuffle, perm, permt, spread, inv, wk, wa, wb, inner, outer, turned_mask,
    s1, r1, tmp, s2, r2, mix, s3, r3, s4, r4, ym, xt, s5, r5,
    acoef, ucoef, table, weighted, plain_t,
    lsem, wsend, wrecv, asend, arecv, bsend, brecv,
    s1s, s1r, s2s, s2r, s3s, s3r, s4s, s4r, s5s, s5r,
):
    lat, ch = lax.axis_index("lat"), lax.axis_index("chan")
    zl, yx = lat // YX, lax.rem(lat, YX)
    active = lax.rem(ch, 4) != 3
    slot = ch - ch // 4
    me_z = zl * CH + ch
    me_slot = zl * SLOTS + slot

    def chan_of(s):
        return s + s // 3

    def z_peer(i):
        return (i // CH) * YX + yx, lax.rem(i, CH)

    def z_holder(i):
        return (i // SLOTS) * YX + yx, chan_of(lax.rem(i, SLOTS))

    def xy_peer(i):
        return zl * YX + i, ch

    def chan_peer(i):
        return lat, i

    def chan_holder(i):
        return lat, chan_of(i)

    def send(n, start, peer, src, dst, ssem, rsem):
        def body(i, carry):
            t = lax.rem(i + start, n)
            to = peer(t)
            mine = (to[0] == lat) & (to[1] == ch)

            @pl.when(jnp.logical_not(mine))
            def _():
                pltpu.make_async_remote_copy(
                    src_ref=src(t), dst_ref=dst, send_sem=ssem, recv_sem=rsem,
                    device_id=to, device_id_type=pl.DeviceIdType.MESH,
                ).start()

            @pl.when(mine)
            def _():
                pltpu.make_async_copy(src(t), dst, rsem).start()

            return carry

        lax.fori_loop(0, n, body, 0)

    def wait(ref, sem):
        pltpu.make_async_copy(ref, ref, sem).wait()

    loads = [
        pltpu.make_async_copy(a, b, lsem.at[k])
        for k, (a, b) in enumerate(
            (
                (x_h, x), (fwd_h, fwd), (shuffle_h, shuffle), (aux_h, aux), (spread_h, spread),
                (perm_h, perm), (permt_h, permt), (inv_h, inv),
            )
        )
    ]
    for load in loads[:4]:
        load.start()

    barrier = pltpu.get_barrier_semaphore()

    def greet(n, peer):
        def body(i, carry):
            to = peer(i)

            @pl.when((to[0] != lat) | (to[1] != ch))
            def _():
                pl.semaphore_signal(
                    barrier, inc=1, device_id=to, device_id_type=pl.DeviceIdType.MESH
                )

            return carry

        lax.fori_loop(0, n, body, 0)

    greet(ZL * CH, z_peer)
    greet(YX, xy_peer)
    for load in loads[4:]:
        load.start()

    natural = lax.broadcasted_iota(jnp.int32, (MODES, MODES), 0)
    orders = ord_v[...].reshape(1, MODES)
    one_hot = jnp.where(natural == orders, 1.0, 0.0).astype(BF)
    loads[2].wait()
    select = dot(shuffle[...], one_hot, 1, 1).astype(BF)
    loads[0].wait()
    loads[1].wait()
    parts = [dot(fwd[k * MODES : (k + 1) * MODES, :], x[...], 1, 1) for k in range(2)]
    wide = PAIR * CHANS
    coeffs = jnp.concatenate(
        [parts[p][:, g * wide : (g + 1) * wide] for g in range(GROUPS) for p in range(2)], axis=1
    ).astype(BF)
    chosen = dot(select, coeffs).astype(BF)
    for g in range(GROUPS):
        lanes = slice(g * LANES, (g + 1) * LANES)
        s1[g] = chosen[:, lanes].reshape(ZL * SLOTS, YX, LANES)

    pl.semaphore_wait(barrier, ZL * CH - 1 + YX - 1)

    def send_mixing(p):
        send(SLOTS, lax.rem(ch, SLOTS), chan_holder,
             lambda t: w_h.at[t, p], wk.at[p, ch], wsend.at[p], wrecv.at[p])

    for g in range(GROUPS):
        send(ZL * SLOTS, zl * SLOTS + lax.rem(ch, SLOTS), z_holder,
             lambda t: s1.at[g, t], r1.at[g, me_z], s1s.at[g], s1r.at[g])
    tile_row = pl.multiple_of(lax.rem(yx // 2, 4) * 16, 16)
    tile_lane = pl.multiple_of(lax.rem(yx, 2) * 128, 128)

    @pl.when(yx < TILES // 2)
    def _():
        send(CH, ch, chan_peer, lambda t: inner_h.at[pl.ds(tile_row, 16), pl.ds(tile_lane, 128)],
             wa.at[ch], asend, arecv)

    @pl.when(yx >= TILES // 2)
    def _():
        send(CH, ch, chan_peer, lambda t: outer_h.at[pl.ds(tile_row, 16), pl.ds(tile_lane, 128)],
             wa.at[ch], asend, arecv)

    send_mixing(0)

    loads[4].wait()
    moved = [dot(spread[half], x[...], 1, 1) for half in range(2)]
    for g in range(GROUPS):
        xt[g] = jnp.concatenate(
            [moved[half][:, g * wide : (g + 1) * wide] for half in range(2)], axis=1
        ).astype(BF)
    loads[3].wait()
    padded = jnp.concatenate([mask[...].astype(F32), jnp.zeros((ROWS, 76), F32)], axis=1)
    padded = jnp.concatenate([padded, jnp.zeros((8 - ROWS, 256), F32)], axis=0)
    turned_mask[...] = padded.T

    @pl.when(active)
    def _():
        held = lax.broadcasted_iota(jnp.int32, (1, MODES), 1) == lat * SLOTS + slot
        order = jnp.sum(jnp.where(held, orders.astype(F32), 0.0), axis=1, keepdims=True)
        i = lax.broadcasted_iota(jnp.int32, (MODES, 128), 0).astype(F32)
        later = i >= 1.0
        degree = order + i
        low = i - 1.0
        prev = degree - 1.0
        a = jnp.sqrt(
            (4.0 * degree * degree - 1.0) / jnp.where(later, i * (2.0 * order + i), 1.0)
        )
        b = jnp.sqrt(
            jnp.maximum(low * (2.0 * order + low), 0.0)
            / jnp.maximum(4.0 * prev * prev - 1.0, 1.0)
        )
        acoef[...] = jnp.where(later, a, 0.0)
        ucoef[...] = jnp.where(later, a * b, 1.0)
        m_of = lax.broadcasted_iota(jnp.int32, (1, MODES), 1).astype(F32)
        picked = jnp.sum(
            jnp.where(m_of == order, aux[24:25, :MODES], 0.0), axis=1, keepdims=True
        )
        cosine = aux[0:8, :128]
        log_first = order * aux[8:16, :128] + (picked + 0.5 * math.log(0.5))

        def steps(t, carry):
            one, two, log_now = carry
            factor = jnp.exp(log_now)
            for s in range(8):
                k = t * 8 + s
                now = acoef[pl.ds(k, 1), :] * cosine * one - ucoef[pl.ds(k, 1), :] * two
                table[pl.ds(pl.multiple_of(k * 8, 8), 8), :] = now * factor
                one, two = now, one
            big = jnp.maximum(jnp.abs(one), jnp.abs(two)) > 2.0**40
            shrink = jnp.where(big, 2.0**-40, 1.0)
            log_now = log_now + jnp.where(big, 40.0 * math.log(2.0), 0.0)
            return one * shrink, two * shrink, log_now

        lax.fori_loop(
            0, MODES // 8, steps,
            (jnp.zeros((8, 128), F32), jnp.full((8, 128), -1.0, F32), log_first),
        )
        valid = i < MODES - order
        for k in range(GROUPS * WIDE // 128):
            lanes = slice(k * 128, (k + 1) * 128)
            part = jnp.where(valid, table[pl.ds(k, MODES, stride=8), :], 0.0)
            for p in range(2):
                weighted[p, :, lanes] = (part * aux[16 + p : 17 + p, lanes]).astype(BF)
            turned = part.T
            row = lax.broadcasted_iota(jnp.int32, (128, MODES), 0)
            which = lax.rem(row // (BLOCK // 2), 2)
            for p in range(2):
                plain_t[lanes, p * MODES : (p + 1) * MODES] = jnp.where(
                    which == p, turned, 0.0
                ).astype(BF)

    wait(wa, arecv)
    send(YX, yx, xy_peer, lambda t: wa, wb.at[yx], bsend, brecv)
    loads[5].wait()
    loads[6].wait()

    @pl.when(active)
    def _():
        for g in range(GROUPS):
            wait(r1.at[g], s1r.at[g])
            blocks = [
                jnp.concatenate([r1[g, z * CH + c] for z in range(ZL)], axis=0)
                for c in range(CH)
            ]
            for k in range(2 * PAIR):
                tmp[k * ZL * YX : (k + 1) * ZL * YX, :] = jnp.concatenate(
                    [blocks[c][:, k * CHANS : (k + 1) * CHANS] for c in range(CH)], axis=1
                )
            s2[g] = dot(perm[...], tmp[...]).astype(BF).reshape(YX, BLOCK, FULL)
            send(YX, yx, xy_peer, lambda t: s2.at[g, t], r2.at[g, yx], s2s.at[g], s2r.at[g])

    send_mixing(1)

    @pl.when(active)
    def _():
        spectra = [0.0, 0.0]
        for g in range(GROUPS):
            wait(r2.at[g], s2r.at[g])
            field = r2[g].reshape(WIDE, FULL)
            for p in range(2):
                spectra[p] += dot(weighted[p, :, g * WIDE : (g + 1) * WIDE], field)
        real, imag = (v.astype(BF) for v in spectra)
        for p in range(2):
            wait(wk.at[p], wrecv.at[p])
        w_real = wk[0].reshape(FULL, FULL)
        w_imag = wk[1].reshape(FULL, FULL)
        mix[0:MODES, :] = (dot(real, w_real, 1, 1) - dot(imag, w_imag, 1, 1)).astype(BF)
        mix[MODES:, :] = (dot(real, w_imag, 1, 1) + dot(imag, w_real, 1, 1)).astype(BF)
        for g in range(GROUPS):
            rows = slice(g * WIDE, (g + 1) * WIDE)
            s3[g] = dot(plain_t[rows, :], mix[...]).astype(BF).reshape(YX, BLOCK, FULL)
            send(YX, yx, xy_peer, lambda t: s3.at[g, t], r3.at[g, yx], s3s.at[g], s3r.at[g])
        for g in range(GROUPS):
            wait(r3.at[g], s3r.at[g])
            back = dot(permt[...], r3[g].reshape(WIDE, FULL)).astype(BF)
            for c in range(CH):
                piece = jnp.concatenate(
                    [
                        back[k * ZL * YX : (k + 1) * ZL * YX, c * CHANS : (c + 1) * CHANS]
                        for k in range(2 * PAIR)
                    ],
                    axis=1,
                )
                for z in range(ZL):
                    s4[g, z * CH + c] = piece[z * YX : (z + 1) * YX, :]
            send(ZL * CH, me_z, z_peer,
                 lambda t: s4.at[g, t], r4.at[g, me_slot], s4s.at[g], s4r.at[g])

    unselect = dot(one_hot, shuffle[...], 1, 1).astype(BF)
    wait(wb, brecv)
    for t in range(TILES):
        whole = inner if t < TILES // 2 else outer
        a, b = (t // 2) % 4 * 16, t % 2 * 128
        whole[:, a : a + 16, b : b + 128] = wb[t]
    loads[7].wait()
    for g in range(GROUPS):
        wait(r4.at[g], s4r.at[g])
        held = dot(unselect, r4[g].reshape(MODES, LANES)).astype(BF)
        ym[0:MODES, :] = held[:, :wide]
        ym[MODES:, :] = held[:, wide:]
        both = jnp.concatenate([dot(inv[half], ym[...]) for half in range(2)], axis=1)
        s5[g] = (both + xt[g].astype(F32)).astype(BF).reshape(CH, PTS, LANES)
        send(CH, ch, chan_peer, lambda t: s5.at[g, t], r5.at[g, ch], s5s.at[g], s5r.at[g])

    inner_all = inner[...].reshape(FFN, FULL)
    outer_all = outer[...].reshape(FFN, FULL)
    for g in range(GROUPS):
        wait(r5.at[g], s5r.at[g])
        hidden = jnp.concatenate(
            [
                jnp.concatenate(
                    [r5[g, c, :, k * CHANS : (k + 1) * CHANS] for c in range(CH)], axis=1
                )
                for k in range(2 * PAIR)
            ],
            axis=0,
        )
        activated = jax.nn.gelu(dot(hidden, inner_all, 1, 1)).astype(BF)
        total = hidden.astype(F32) + dot(activated, outer_all)
        for r in range(PAIR):
            row = PAIR * g + r
            points = jnp.concatenate(
                [
                    total[(half * PAIR + r) * PTS : (half * PAIR + r) * PTS + HALF, :]
                    for half in range(2)
                ],
                axis=0,
            )
            out[row] = (points * turned_mask[0 : 2 * HALF, row : row + 1]).astype(BF)

    for p in range(2):
        others = w_h.at[pl.ds(0, SLOTS - 1), p]

        @pl.when(active)
        def _():
            wait(others, wsend.at[p])

        @pl.when(jnp.logical_not(active))
        def _():
            wait(w_h.at[:, p], wsend.at[p])

    wait(wa.at[pl.ds(0, CH - 1)], asend)
    wait(wb.at[pl.ds(0, YX - 1)], bsend)
    for g in range(GROUPS):
        wait(s5.at[g, pl.ds(0, CH - 1)], s5s.at[g])

        @pl.when(active)
        def _():
            wait(s1.at[g, pl.ds(0, ZL * SLOTS - 1)], s1s.at[g])
            wait(s2.at[g, pl.ds(0, YX - 1)], s2s.at[g])
            wait(s3.at[g, pl.ds(0, YX - 1)], s3s.at[g])
            wait(s4.at[g, pl.ds(0, ZL * CH - 1)], s4s.at[g])

        @pl.when(jnp.logical_not(active))
        def _():
            wait(s1.at[g], s1s.at[g])


def local(ocean_state, land_mask, order_table, spectral_weight, inner_weight, outer_weight):
    fwd, inv, spread, perm, permt, shuffle, aux = constants()
    flat_state = ocean_state.reshape(ROWS * CHANS, NLON)
    vmem = pl.BlockSpec(memory_space=pltpu.VMEM)
    anywhere = pl.BlockSpec(memory_space=pl.ANY)
    sem = pltpu.SemaphoreType.DMA
    z_out, z_in = (ZL * SLOTS, YX, LANES), (ZL * CH, YX, LANES)

    def held(*shape):
        return pltpu.VMEM(shape, BF)

    return pl.pallas_call(
        layer,
        out_shape=jax.ShapeDtypeStruct((ROWS, 2 * HALF, FULL), BF),
        in_specs=[vmem] * 2 + [anywhere] * 11,
        out_specs=vmem,
        scratch_shapes=[
            held(*flat_state.shape),
            pltpu.VMEM(aux.shape, F32),
            held(*fwd.shape),
            held(*shuffle.shape),
            held(*perm.shape),
            held(*perm.shape),
            held(*spread.shape),
            held(*inv.shape),
            held(2, CH, CHANS, FULL),
            held(CH, 16, 128),
            held(YX, CH, 16, 128),
            held(CH, FFN // CH, FULL),
            held(CH, FFN // CH, FULL),
            pltpu.VMEM((256, 8), F32),
            held(GROUPS, *z_out),
            held(GROUPS, *z_in),
            held(WIDE, FULL),
            held(GROUPS, YX, BLOCK, FULL),
            held(GROUPS, YX, BLOCK, FULL),
            held(2 * MODES, FULL),
            held(GROUPS, YX, BLOCK, FULL),
            held(GROUPS, YX, BLOCK, FULL),
            held(GROUPS, *z_in),
            held(GROUPS, *z_out),
            held(2 * MODES, LANES // 2),
            held(GROUPS, CH * PTS, LANES),
            held(GROUPS, CH, PTS, LANES),
            held(GROUPS, CH, PTS, LANES),
            pltpu.VMEM((MODES, 128), F32),
            pltpu.VMEM((MODES, 128), F32),
            pltpu.VMEM((MODES * 8, 128), F32),
            held(2, MODES, GROUPS * WIDE),
            held(GROUPS * WIDE, 2 * MODES),
            sem((8,)),
            sem((2,)),
            sem((2,)),
            sem,
            sem,
            sem,
            sem,
        ]
        + [sem((GROUPS,))] * 10,
        compiler_params=pltpu.CompilerParams(
            collective_id=0, has_side_effects=True, vmem_limit_bytes=60 * 2**20
        ),
        cost_estimate=pl.CostEstimate(
            flops=2 * 10**9, bytes_accessed=12 * 10**6, transcendentals=10**5
        ),
    )(
        order_table, land_mask, flat_state, aux, fwd, shuffle, perm, permt, spread, inv,
        spectral_weight, inner_weight.T, outer_weight,
    )


def solution(mesh):
    placed = (
        P("lat", "chan", None),
        P("lat", "chan"),
        P(),
        P("lat", None, "chan", None),
        P(None, "chan"),
        P("chan", None),
    )
    return jax.shard_map(
        local, mesh=mesh, in_specs=placed, out_specs=P("lat", "chan", None), check_vma=False
    )
```

time: 141 us -> 109 us (0.77)
  blocking collectives: 18.2 us -> 0 us
  local copies, waits for them, and re-layouts: 9.1 us -> 1.9 us
  Pallas kernels: 111 us -> 107 us
    all_gather x1 -> x0, blocking collectives: 18.2 us -> none  [local(): weights = lax.all_gather(own, 'chan', axis=0)]
    unnamed x22 -> x1, local copies, waits for them, and re-layouts: 7.86 us -> 1.9 us
    pallas_call x2 -> x1, Pallas kernels: 111 us -> 107 us  [local(): pl.pallas_call(layer, out_shape=jax.ShapeDtypeStruct((ROWS, 2 * HALF, FUL...]
where the time goes in v2:
time: 109 us
  Pallas kernels  107 us (98%)
  local copies, waits for them, and re-layouts  1.9 us (2%)
    pallas_call x1, Pallas kernels, local(): pl.pallas_call(layer, out_shape=jax.ShapeDtypeStruct((ROWS, 2 * HALF, FUL...  107 us

profile of v2, /device:TPU:1, one launch (start us, length us, event | category | flops | bytes accessed | tf_op | source)
XLA Modules:
  0.0 108.5 jit_solution(2559181134971772517)
XLA Ops:
  0.0 106.6 %shard_map.127 = bf16[6,180,256]{2,1,0:T(8,128)(2,1)} custom-call(s32[384]{0:T(512)} %ord_v.1, s32[6,180]{1,0:T(8,128)} %mask.1, bf16[192,1440]{1,0:T(8,128)(2,1)} %bitcast.2, f32[32,768]{1,0:T(8,128)} %constant.14.clone.aux_h, bf16[768,1440]{1,0:T(8,128)(2,1)} %constant.15.clone.fwd_h, bf16[384,384]{1,0:T(8,128)(2,1)} %constant.16.clone.shuffle_h, ...), custom_call_target="tpu_custom_call" | custom-call | flops 2000000000 | bytes 12000000 | tf_op jit(solution)/shard_map/pallas_call | solution.py:421
  106.6 1.9 %copy.15 = bf16[6,180,256]{2,1,0:T(8,128)(2,1)} copy(bf16[6,180,256]{2,1,0:T(8,128)(2,1)} %shard_map.127) | data formatting | bytes 1105920

commit v3 on v2

--- a/solution.py
+++ b/solution.py
@@ -106,6 +106,12 @@
     def z_holder(i):
         return (i // SLOTS) * YX + yx, chan_of(lax.rem(i, SLOTS))
 
+    def z_far_first(i):
+        t, core = i // 2, lax.rem(i, 2)
+        away = 8 + (t + 1) // 2 * (1 - 2 * lax.rem(t, 2))
+        z = lax.rem(ch // 2 * ZL + zl + away, 16)
+        return lax.rem(z, ZL) * YX + yx, z // ZL * 2 + core
+
     def xy_peer(i):
         return zl * YX + i, ch
 
@@ -167,7 +173,7 @@
 
         lax.fori_loop(0, n, body, 0)
 
-    greet(ZL * CH, z_peer)
+    greet(ZL * CH, z_far_first)
     greet(YX, xy_peer)
     for load in loads[4:]:
         load.start()
@@ -211,7 +217,6 @@
         send(CH, ch, chan_peer, lambda t: outer_h.at[pl.ds(tile_row, 16), pl.ds(tile_lane, 128)],
              wa.at[ch], asend, arecv)
 
-    send_mixing(0)
 
     loads[4].wait()
     moved = [dot(spread[half], x[...], 1, 1) for half in range(2)]
@@ -280,10 +285,20 @@
                     which == p, turned, 0.0
                 ).astype(BF)
 
-    wait(wa, arecv)
-    send(YX, yx, xy_peer, lambda t: wa, wb.at[yx], bsend, brecv)
     loads[5].wait()
     loads[6].wait()
+    for g in range(GROUPS):
+
+        @pl.when(active)
+        def _():
+            wait(s1.at[g, pl.ds(0, ZL * SLOTS - 1)], s1s.at[g])
+
+        @pl.when(jnp.logical_not(active))
+        def _():
+            wait(s1.at[g], s1s.at[g])
+
+    send_mixing(0)
+    send_mixing(1)
 
     @pl.when(active)
     def _():
@@ -300,7 +315,6 @@
             s2[g] = dot(perm[...], tmp[...]).astype(BF).reshape(YX, BLOCK, FULL)
             send(YX, yx, xy_peer, lambda t: s2.at[g, t], r2.at[g, yx], s2s.at[g], s2r.at[g])
 
-    send_mixing(1)
 
     @pl.when(active)
     def _():
@@ -337,12 +351,10 @@
             send(ZL * CH, me_z, z_peer,
                  lambda t: s4.at[g, t], r4.at[g, me_slot], s4s.at[g], s4r.at[g])
 
+    wait(wa, arecv)
+    send(YX, yx, xy_peer, lambda t: wa, wb.at[yx], bsend, brecv)
+
     unselect = dot(one_hot, shuffle[...], 1, 1).astype(BF)
-    wait(wb, brecv)
-    for t in range(TILES):
-        whole = inner if t < TILES // 2 else outer
-        a, b = (t // 2) % 4 * 16, t % 2 * 128
-        whole[:, a : a + 16, b : b + 128] = wb[t]
     loads[7].wait()
     for g in range(GROUPS):
         wait(r4.at[g], s4r.at[g])
@@ -353,6 +365,11 @@
         s5[g] = (both + xt[g].astype(F32)).astype(BF).reshape(CH, PTS, LANES)
         send(CH, ch, chan_peer, lambda t: s5.at[g, t], r5.at[g, ch], s5s.at[g], s5r.at[g])
 
+    wait(wb, brecv)
+    for t in range(TILES):
+        whole = inner if t < TILES // 2 else outer
+        a, b = (t // 2) % 4 * 16, t % 2 * 128
+        whole[:, a : a + 16, b : b + 128] = wb[t]
     inner_all = inner[...].reshape(FFN, FULL)
     outer_all = outer[...].reshape(FFN, FULL)
     for g in range(GROUPS):
@@ -397,14 +414,9 @@
 
         @pl.when(active)
         def _():
-            wait(s1.at[g, pl.ds(0, ZL * SLOTS - 1)], s1s.at[g])
             wait(s2.at[g, pl.ds(0, YX - 1)], s2s.at[g])
             wait(s3.at[g, pl.ds(0, YX - 1)], s3s.at[g])
             wait(s4.at[g, pl.ds(0, ZL * CH - 1)], s4s.at[g])
-
-        @pl.when(jnp.logical_not(active))
-        def _():
-            wait(s1.at[g], s1s.at[g])
 
 
 def local(ocean_state, land_mask, order_table, spectral_weight, inner_weight, outer_weight):

time: 109 us -> 101 us (0.927)
  the two profiles are of different devices: /device:TPU:1 before, /device:TPU:65 now
where the time goes in v3:
time: 101 us
  Pallas kernels  99.2 us (98%)
  local copies, waits for them, and re-layouts  1.9 us (2%)
    pallas_call x1, Pallas kernels, local(): pl.pallas_call(layer, out_shape=jax.ShapeDtypeStruct((ROWS, 2 * HALF, FUL...  99.2 us

profile of v3, /device:TPU:65, one launch (start us, length us, event | category | flops | bytes accessed | tf_op | source)
XLA Modules:
  0.0 101.2 jit_solution(9755717284221955290)
XLA Ops:
  0.0 99.2 %shard_map.127 = bf16[6,180,256]{2,1,0:T(8,128)(2,1)} custom-call(s32[384]{0:T(512)} %ord_v.1, s32[6,180]{1,0:T(8,128)} %mask.1, bf16[192,1440]{1,0:T(8,128)(2,1)} %bitcast.2, f32[32,768]{1,0:T(8,128)} %constant.14.clone.aux_h, bf16[768,1440]{1,0:T(8,128)(2,1)} %constant.15.clone.fwd_h, bf16[384,384]{1,0:T(8,128)(2,1)} %constant.16.clone.shuffle_h, ...), custom_call_target="tpu_custom_call" | custom-call | flops 2000000000 | bytes 12000000 | tf_op jit(solution)/shard_map/pallas_call | solution.py:433
  99.3 1.9 %copy.15 = bf16[6,180,256]{2,1,0:T(8,128)(2,1)} copy(bf16[6,180,256]{2,1,0:T(8,128)(2,1)} %shard_map.127) | data formatting | bytes 1105920

commit v4 on v3

--- a/solution.py
+++ b/solution.py
@@ -92,19 +92,20 @@
 ):
     lat, ch = lax.axis_index("lat"), lax.axis_index("chan")
     zl, yx = lat // YX, lax.rem(lat, YX)
-    active = lax.rem(ch, 4) != 3
-    slot = ch - ch // 4
+    odd = lax.rem(zl, 2)
+    active = lax.rem(ch, 4) != 3 - 2 * odd
+    slot = ch - (ch + 2 * odd) // 4
     me_z = zl * CH + ch
     me_slot = zl * SLOTS + slot
 
-    def chan_of(s):
-        return s + s // 3
+    def chan_of(s, z):
+        return s + (s + 2 * lax.rem(z, 2)) // 3
 
     def z_peer(i):
         return (i // CH) * YX + yx, lax.rem(i, CH)
 
     def z_holder(i):
-        return (i // SLOTS) * YX + yx, chan_of(lax.rem(i, SLOTS))
+        return (i // SLOTS) * YX + yx, chan_of(lax.rem(i, SLOTS), i // SLOTS)
 
     def z_far_first(i):
         t, core = i // 2, lax.rem(i, 2)
@@ -119,7 +120,7 @@
         return lat, i
 
     def chan_holder(i):
-        return lat, chan_of(i)
+        return lat, chan_of(i, zl)
 
     def send(n, start, peer, src, dst, ssem, rsem):
         def body(i, carry):
@@ -351,13 +352,13 @@
             send(ZL * CH, me_z, z_peer,
                  lambda t: s4.at[g, t], r4.at[g, me_slot], s4s.at[g], s4r.at[g])
 
-    wait(wa, arecv)
-    send(YX, yx, xy_peer, lambda t: wa, wb.at[yx], bsend, brecv)
-
     unselect = dot(one_hot, shuffle[...], 1, 1).astype(BF)
     loads[7].wait()
     for g in range(GROUPS):
         wait(r4.at[g], s4r.at[g])
+        if g == 0:
+            wait(wa, arecv)
+            send(YX, yx, xy_peer, lambda t: wa, wb.at[yx], bsend, brecv)
         held = dot(unselect, r4[g].reshape(MODES, LANES)).astype(BF)
         ym[0:MODES, :] = held[:, :wide]
         ym[MODES:, :] = held[:, wide:]

time: 101 us -> 98.6 us (0.976)
  the two profiles are of different devices: /device:TPU:65 before, /device:TPU:33 now
where the time goes in v4:
time: 98.6 us; the launch traced here: 98.5 us
  Pallas kernels  96.5 us (98%)
  local copies, waits for them, and re-layouts  1.9 us (2%)
    pallas_call x1, Pallas kernels, local(): pl.pallas_call(layer, out_shape=jax.ShapeDtypeStruct((ROWS, 2 * HALF, FUL...  96.5 us

profile of v4, /device:TPU:33, one launch (start us, length us, event | category | flops | bytes accessed | tf_op | source)
XLA Modules:
  0.0 98.5 jit_solution(10922144178567729708)
XLA Ops:
  0.0 96.5 %shard_map.127 = bf16[6,180,256]{2,1,0:T(8,128)(2,1)} custom-call(s32[384]{0:T(512)} %ord_v.1, s32[6,180]{1,0:T(8,128)} %mask.1, bf16[192,1440]{1,0:T(8,128)(2,1)} %bitcast.2, f32[32,768]{1,0:T(8,128)} %constant.14.clone.aux_h, bf16[768,1440]{1,0:T(8,128)(2,1)} %constant.15.clone.fwd_h, bf16[384,384]{1,0:T(8,128)(2,1)} %constant.16.clone.shuffle_h, ...), custom_call_target="tpu_custom_call" | custom-call | flops 2000000000 | bytes 12000000 | tf_op jit(solution)/shard_map/pallas_call | solution.py:434
  96.6 1.9 %copy.15 = bf16[6,180,256]{2,1,0:T(8,128)(2,1)} copy(bf16[6,180,256]{2,1,0:T(8,128)(2,1)} %shard_map.127) | data formatting | bytes 1105920
